TPU v7x, 256 devices: a whole 4x4x8 slice. The times are simulated.
256 devices in a mesh: qb: 16 (over z, core), kb: 16 (over y, x).
Axes of the slice: x: 4, y: 4, z: 8, core: 2. Of those that a mesh axis runs over, the one named last changes fastest.
Arguments:
- queries: float32 [16384, 1024], P(('qb', 'kb')), may hold values from -300 to 300
- keys: float32 [16384, 128], P(('qb', 'kb')), may hold values from -7 to 7, as said below
- values: float32 [16384, 128], P(('qb', 'kb')), may hold values from -6 to 6
- block_mask: int32 [512, 512], replicated, may hold values 0 or 1
- key_lengths: int32 [16384], replicated, may hold values from 1 to 16384, as said below
Outputs:
- attended: float32 [16384, 1024], P(('qb', 'kb'))
- log_norm: float32 [8, 16384], P(None, ('qb', 'kb'))
Inputs may be any that keep to these rules, and one draw needn't show every extreme that they name: keys are of order one. key_lengths[r] lies between min(r + 1, 64) and r + 1; the last row has 16384.
All inputs are finite; a program needn't handle non-finite values.
Results may differ from a plain program's by a relative error of at most 0.0003.
Values sent between devices are 32-bit elements; how exact they have to be, the bound alone decides.
A program may use at most 64 MiB of HBM per device.

v0:
```python
import jax
import jax.numpy as jnp
from jax import lax
from jax.sharding import PartitionSpec as P

HEADS = 8
HEAD_DIM = 128
MBLK = 32


NEG = -1e30


def tile_mask(q_pos, k_pos, q_start, block_mask, key_lengths):
    rows = q_pos.shape[0]
    lengths = lax.dynamic_slice_in_dim(key_lengths, q_start, rows, 0)
    mask_rows = lax.dynamic_slice_in_dim(block_mask, q_start // MBLK, rows // MBLK, 0)
    column_ids = jnp.arange(block_mask.shape[1], dtype=jnp.int32)
    picks = (column_ids[:, None] == k_pos[None, :] // MBLK).astype(jnp.float32)
    coarse = jnp.dot(mask_rows.astype(jnp.float32), picks, precision=lax.Precision.HIGHEST) > 0.5
    spread = jnp.repeat(coarse, MBLK, axis=0)
    same = q_pos[:, None] // MBLK == k_pos[None, :] // MBLK
    diff = q_pos[:, None] - k_pos[None, :]
    return (diff >= 0) & (diff < lengths[:, None]) & (spread | same)


def attend(q_block, k_piece, v_piece, allowed):
    rows = q_block.shape[0]
    width_k = k_piece.shape[0]
    row_step = min(rows, 512)
    row_groups = rows // row_step
    scale = 1.0 / HEAD_DIM**0.5
    per_head = q_block.reshape(row_groups, row_step, HEADS, HEAD_DIM)
    per_head = jnp.transpose(per_head, (2, 0, 1, 3)).reshape(HEADS * row_groups, row_step, HEAD_DIM)
    mask_groups = allowed.reshape(row_groups, row_step, width_k)

    def one_item(item):
        number, q_rows = item
        mask = mask_groups[number % row_groups]
        score = jnp.dot(q_rows, k_piece.T, precision=lax.Precision.HIGHEST) * scale
        masked = jnp.where(mask, score, NEG)
        row_max = jnp.max(masked, axis=1)
        weight = jnp.where(mask, jnp.exp(masked - row_max[:, None]), 0.0)
        total = jnp.sum(weight, axis=1)
        partial_value = jnp.dot(weight, v_piece, precision=lax.Precision.HIGHEST)
        return (partial_value, row_max, total)

    numbers = jnp.arange(HEADS * row_groups, dtype=jnp.int32)
    partial_value, row_max, total = lax.map(one_item, (numbers, per_head))
    partial_value = partial_value.reshape(HEADS, row_groups, row_step, HEAD_DIM)
    partial_value = jnp.transpose(partial_value, (1, 2, 0, 3)).reshape(rows, HEADS * HEAD_DIM)
    return (partial_value, row_max.reshape(HEADS, rows), total.reshape(HEADS, rows))


def rescale(partial_value, factor):
    rows = partial_value.shape[0]
    shaped = partial_value.reshape(rows, HEADS, HEAD_DIM) * jnp.transpose(factor)[:, :, None]
    return shaped.reshape(rows, HEADS * HEAD_DIM)


def shards(queries, keys, values, block_mask, key_lengths):
    tok_dev = queries.shape[0]
    q_rank = lax.axis_index("qb")
    k_rank = lax.axis_index("kb")
    q_block = lax.all_gather(queries, "kb", axis=0, tiled=True)
    k_block, v_block = (
        lax.all_gather(keys, "qb", axis=0, tiled=True),
        lax.all_gather(values, "qb", axis=0, tiled=True),
    )
    rows = q_block.shape[0]
    width_k = k_block.shape[0]
    q_start = q_rank * rows
    spots = jnp.arange(width_k, dtype=jnp.int32)
    k_pos = spots // tok_dev * rows + k_rank * tok_dev + spots % tok_dev
    q_pos = q_start + jnp.arange(rows, dtype=jnp.int32)
    allowed = tile_mask(q_pos, k_pos, q_start, block_mask, key_lengths)
    partial_value, row_max, total = attend(q_block, k_block, v_block, allowed)
    global_max = lax.pmax(row_max, "kb")
    factor = jnp.exp(row_max - global_max)
    scaled = rescale(partial_value, factor)
    scaled_total = jnp.transpose(total * factor)
    out_sum, total_sum = (
        lax.psum_scatter(scaled, "kb", scatter_dimension=0, tiled=True),
        lax.psum_scatter(scaled_total, "kb", scatter_dimension=0, tiled=True),
    )
    own_max = lax.dynamic_slice_in_dim(global_max, k_rank * tok_dev, tok_dev, 1)
    attended = (out_sum.reshape(tok_dev, HEADS, HEAD_DIM) / total_sum[:, :, None]).reshape(
        tok_dev, HEADS * HEAD_DIM
    )
    log_norm = own_max + jnp.log(jnp.transpose(total_sum))
    return (attended, log_norm)


def solution(mesh):
    in_specs = (P(("qb", "kb"), None), P(("qb", "kb"), None), P(("qb", "kb"), None), P(), P())
    out_specs = (P(("qb", "kb"), None), P(None, ("qb", "kb")))
    return jax.shard_map(shards, mesh=mesh, in_specs=in_specs, out_specs=out_specs, check_vma=False)
```

profile of v0, /device:TPU:224, one launch (start us, length us, event | category | flops | bytes accessed | tf_op | source)
XLA Modules:
  0.0 468.5 jit_solution(4166965004816046667)
XLA Ops:
  8.7 1.7 fusion.18
  10.5 15.6 %all_gather.10 = f32[1024,128]{1,0:T(8,128)S(1)} all-gather(f32[64,128]{1,0:T(8,128)} %param.8), channel_id=1, replica_groups=mesh['qb'=16,'kb'=16] {'qb'}, dimensions={0}, use_global_device_ids=true | all-gather | bytes 557056 | tf_op jit(solution)/shard_map/all_gather | solution.py:67
  26.1 18.0 %all_gather.11 = f32[1024,128]{1,0:T(8,128)S(1)} all-gather(f32[64,128]{1,0:T(8,128)} %param.9), channel_id=1, replica_groups=mesh['qb'=16,'kb'=16] {'qb'}, dimensions={0}, use_global_device_ids=true | all-gather | bytes 557056 | tf_op jit(solution)/shard_map/all_gather | solution.py:68
  44.3 1.9 fusion.16
  46.2 21.2 %all-gather.2.cloned.1.call-done = f32[1024,1024]{1,0:T(8,128)} async-done(((f32[64,1024]{1,0:T(8,128)}), f32[1024,1024]{1,0:T(8,128)}) %all-gather.2.cloned.1.call-update) | async-done | bytes 4194320 | tf_op jit(solution)/shard_map/all_gather | solution.py:65
  67.4 3.2 copy.17
  70.6 2.7 copy.11
  73.3 152.5 %while.16 = (s32[]{:T(128)}, f32[16,512,128]{2,1,0:T(8,128)}, f32[16,512]{1,0:T(8,128)S(1)}, f32[16,512]{1,0:T(8,128)S(1)}, s32[16]{0:T(128)S(1)}, /*index=5*/pr...) while((s32[]{:T(128)}, f32[16,512,128]{2,1,0:T(8,128)}, ...), condition=%wide.region_3.4_spmd, body=%wide.region_0.3_spmd.sunk | while | flops 1616903168 | bytes 9454884 | solution.py:49
  75.9 3.1 fusion.45
  79.0 2.9 fusion.46
  81.9 0.8 fusion.47
  85.4 3.1 fusion.45
  88.5 3.0 fusion.46
  91.4 0.8 fusion.47
  94.9 3.1 fusion.45
  98.0 3.0 fusion.46
  101.0 0.8 fusion.47
  104.4 3.1 fusion.45
  107.5 3.0 fusion.46
  110.5 0.8 fusion.47
  114.0 3.1 fusion.45
  117.1 3.0 fusion.46
  120.0 0.8 fusion.47
  123.5 3.1 fusion.45
  126.6 3.0 fusion.46
  129.6 0.8 fusion.47
  133.1 3.1 fusion.45
  136.1 3.0 fusion.46
  139.1 0.8 fusion.47
  142.6 3.1 fusion.45
  145.7 3.0 fusion.46
  148.6 0.8 fusion.47
  152.1 3.1 fusion.45
  155.2 3.0 fusion.46
  158.2 0.8 fusion.47
  161.6 3.1 fusion.45
  164.7 3.0 fusion.46
  167.7 0.8 fusion.47
  171.2 3.1 fusion.45
  174.3 3.0 fusion.46
  177.2 0.8 fusion.47
  180.7 3.1 fusion.45
  183.8 3.0 fusion.46
  186.8 0.8 fusion.47
  190.3 3.1 fusion.45
  193.3 3.0 fusion.46
  196.3 0.8 fusion.47
  199.8 3.1 fusion.45
  202.9 2.9 fusion.46
  209.3 3.1 fusion.45
  212.4 3.0 fusion.46
  215.3 0.8 fusion.47
  218.8 3.1 fusion.45
  221.9 3.0 fusion.46
  225.8 72.4 %pmax.7 = f32[8,1024]{1,0:T(8,128)S(1)} all-reduce(f32[8,1024]{1,0:T(8,128)S(1)} %reshape.160), channel_id=1, replica_groups=mesh['qb'=16,'kb'=16] {'kb'}, use_global_device_ids=true, to_apply=%region_4.5 | all-reduce | flops 8192 | bytes 65536 | tf_op jit(solution)/shard_map/pmax | solution.py:78
  298.2 1.1 copy.15
  299.7 4.6 copy.12
  304.4 1.1 mul.44
  305.5 4.0 bitcast_multiply_fusion
  309.5 63.6 %reduce-scatter.7.cloned.1.call-done = f32[64,8]{1,0:T(8,128)} async-done(((f32[1024,8]{1,0:T(8,128)}), f32[64,8]{1,0:T(8,128)}) %reduce-scatter.7.cloned.1.call-update) | async-done | bytes 2064 | tf_op jit(solution)/shard_map/reduce_scatter | solution.py:84
  373.2 0.8 copy.16
  374.6 84.7 %reduce-scatter.5.cloned.1.call-done = f32[64,1024]{1,0:T(8,128)} async-done(((f32[1024,1024]{1,0:T(8,128)}), f32[64,1024]{1,0:T(8,128)}) %reduce-scatter.5.cloned.1.call-update) | async-done | bytes 262160 | tf_op jit(solution)/shard_map/reduce_scatter | solution.py:83
  459.4 0.9 div.66
  460.2 1.7 bitcast_divide_fusion
  (70 shorter events, 15.8 us)
Async XLA Ops:
  7.2 60.3 %all-gather.2.cloned.1.call-start = ((), (), s32[]{:S(2)}) async-start(), calls=%async_computation.2 | async-start | bytes 4456448 | tf_op jit(solution)/shard_map/all_gather | solution.py:65
  7.9 365.3 %reduce-scatter.7.cloned.1.call-start = ((), (), s32[]{:S(2)}) async-start(), calls=%async_computation.4 | async-start | bytes 557056 | tf_op jit(solution)/shard_map/reduce_scatter | solution.py:84
  299.3 160.0 %reduce-scatter.5.cloned.1.call-start = ((), (), s32[]{:S(2)}) async-start(), calls=%async_computation.3 | async-start | bytes 4456448 | tf_op jit(solution)/shard_map/reduce_scatter | solution.py:83
Sparse Core Ops, SparseCore 0:
  10.4 56.9 all-gather.1
  299.4 73.6 reduce-scatter.6
  377.2 82.0 reduce-scatter.4
where the time goes:
time: 472 us; the launch traced here: 469 us
  waiting for transfers between devices  170 us (36%)
  blocking collectives  106 us (22%)
  matrix products  98.7 us (21%)
  loops' own time  31.9 us (7%)
  local copies, waits for them, and re-layouts  26.8 us (6%)
  other arithmetic  20.7 us (4%)
  between operations  13.9 us (3%)
    reduce_scatter x1, waiting for transfers between devices, shards(): lax.psum_scatter(scaled, 'kb', scatter_dimension=0, tiled=True)  84.7 us
    pmax x1, blocking collectives, shards(): global_max = lax.pmax(row_max, 'kb')  72.4 us
    reduce_scatter x1, waiting for transfers between devices, shards(): lax.psum_scatter(scaled_total, 'kb', scatter_dimension=0, tiled=True)  63.6 us
    dot_general x16, matrix products, one_item(): score = jnp.dot(q_rows, k_piece.T, precision=lax.Precision.HIGHEST) * scale  49.5 us
    dot_general x16, matrix products, one_item(): partial_value = jnp.dot(weight, v_piece, precision=lax.Precision.HIGHEST)  47.4 us
    another operation x1, loops' own time, attend(): partial_value, row_max, total = lax.map(one_item, (numbers, per_head))  31.9 us
    all_gather x1, waiting for transfers between devices, shards(): q_block = lax.all_gather(queries, 'kb', axis=0, tiled=True)  21.2 us
    all_gather x1, blocking collectives, shards(): lax.all_gather(values, 'qb', axis=0, tiled=True)  18 us
  transfers between devices with their start and end apart: 3, of which 3 were waited for; matrix products, arithmetic and copies ran while one was open for 3% of the time, Pallas kernels for 0%

commit v1 on v0

v1 whole, which is shorter than its diff:
```python
import functools
import math

import jax
import jax.numpy as jnp
from jax import lax
from jax.experimental import pallas as pl
from jax.experimental.pallas import tpu as pltpu
from jax.sharding import PartitionSpec as P

HEADS = 8
HEAD_DIM = 128
TOK = 64
PAIRS = HEADS * TOK
NX, NY, NZ = 4, 4, 8
TILE = 2 * NY * TOK
NEG = -1e30
FLOOR = -1e29
BIG = 1 << 30
MESH = pl.DeviceIdType.MESH
F32 = jnp.float32
BF16 = jnp.bfloat16
KT = 256


def split(x):
    hi = x.astype(BF16)
    lo = (x - hi.astype(F32)).astype(BF16)
    return hi, lo


def kernel(
    q_ref, k_ref, v_ref, bm_ref, kl_ref, out_ref, ln_ref,
    qbuf, qcat, kvbuf, kcat, vcat, s, mx, acc, lacc, osend, lsend, orecv, lrecv, own, bm, lens, cp,
    local_sem, qs, qr, zs, zr, ys, yr, cs, cr, os_, or_, ls_, lr_,
):
    qb = lax.axis_index("qb")
    kb = lax.axis_index("kb")
    z, c = lax.div(qb, 2), lax.rem(qb, 2)
    y, x = lax.div(kb, NX), lax.rem(kb, NX)
    gr = qb * NY + y
    partner = (qb + 1 - 2 * c, kb)

    def at_x(d):
        return (qb, y * NX + lax.rem(x + d, NX))

    def at_y(d):
        return (qb, lax.rem(y + d, NY) * NX + x)

    def at_z(d):
        return (lax.rem(qb + 2 * d, 2 * NZ), kb)

    loads = [
        pltpu.make_async_copy(k_ref, kvbuf.at[0, z, c, y], local_sem.at[0]),
        pltpu.make_async_copy(v_ref, kvbuf.at[1, z, c, y], local_sem.at[1]),
        pltpu.make_async_copy(q_ref, qbuf.at[x], local_sem.at[2]),
        pltpu.make_async_copy(bm_ref.at[pl.ds(pl.multiple_of(gr * 8, 8), 8)], bm, local_sem.at[3]),
        pltpu.make_async_copy(kl_ref.at[pl.ds(pl.multiple_of(qb * 8, 8), 8)], lens, local_sem.at[4]),
    ]
    for copy in loads:
        copy.start()

    barrier = pltpu.get_barrier_semaphore()
    peers = [at_x(d) for d in (1, 2, 3)] + [at_y(d) for d in (1, 2, 3)] + [at_z(d) for d in range(1, NZ)] + [partner]
    for peer in peers:
        pl.semaphore_signal(barrier, inc=1, device_id=peer, device_id_type=MESH)
    for copy in loads:
        copy.wait()
    pl.semaphore_wait(barrier, len(peers))

    def q_copy(d):
        return pltpu.make_async_remote_copy(
            src_ref=qbuf.at[x], dst_ref=qbuf.at[x], send_sem=qs.at[d], recv_sem=qr.at[x],
            device_id=at_x(d), device_id_type=MESH)

    def q_arrival(d):
        src = lax.rem(x + d, NX)
        return pltpu.make_async_remote_copy(
            src_ref=qbuf.at[src], dst_ref=qbuf.at[src], send_sem=qs.at[0], recv_sem=qr.at[src],
            device_id=at_x(d), device_id_type=MESH)

    def z_copy(w, d):
        return pltpu.make_async_remote_copy(
            src_ref=kvbuf.at[w, z, c, y], dst_ref=kvbuf.at[w, z, c, y], send_sem=zs.at[w, d], recv_sem=zr.at[w, z],
            device_id=at_z(d), device_id_type=MESH)

    def z_arrival(w, zz):
        return pltpu.make_async_remote_copy(
            src_ref=kvbuf.at[w, zz, c, y], dst_ref=kvbuf.at[w, zz, c, y], send_sem=zs.at[w, 0], recv_sem=zr.at[w, zz],
            device_id=at_z(1), device_id_type=MESH)

    def y_copy(w, zz, d):
        return pltpu.make_async_remote_copy(
            src_ref=kvbuf.at[w, zz, c, y], dst_ref=kvbuf.at[w, zz, c, y], send_sem=ys.at[w, zz, d], recv_sem=yr.at[w, zz, y],
            device_id=at_y(d), device_id_type=MESH)

    def y_arrival(w, zz, d):
        src = lax.rem(y + d, NY)
        return pltpu.make_async_remote_copy(
            src_ref=kvbuf.at[w, zz, c, src], dst_ref=kvbuf.at[w, zz, c, src], send_sem=ys.at[w, zz, 0],
            recv_sem=yr.at[w, zz, src], device_id=at_y(d), device_id_type=MESH)

    def c_copy(w, zz):
        return pltpu.make_async_remote_copy(
            src_ref=kvbuf.at[w, zz, c], dst_ref=kvbuf.at[w, zz, c], send_sem=cs.at[w, zz], recv_sem=cr.at[w, zz],
            device_id=partner, device_id_type=MESH)

    def c_arrival(w, zz):
        return pltpu.make_async_remote_copy(
            src_ref=kvbuf.at[w, zz, 1 - c], dst_ref=kvbuf.at[w, zz, 1 - c], send_sem=cs.at[w, zz], recv_sem=cr.at[w, zz],
            device_id=partner, device_id_type=MESH)

    def o_copy(d):
        return pltpu.make_async_remote_copy(
            src_ref=osend.at[d - 1], dst_ref=orecv.at[d - 1], send_sem=os_.at[d], recv_sem=or_.at[d],
            device_id=at_x(d), device_id_type=MESH)

    def l_copy(d):
        return pltpu.make_async_remote_copy(
            src_ref=lsend.at[d - 1], dst_ref=lrecv.at[d - 1], send_sem=ls_.at[d], recv_sem=lr_.at[d],
            device_id=at_x(d), device_id_type=MESH)

    def stage_a(w, i):
        zz = z - i

        @pl.when(i > 0)
        def _():
            z_arrival(w, zz).wait_recv()
        for d in (1, 3, 2):
            y_copy(w, zz, d).start()

    def stage_b(w, i):
        zz = z - i
        for d in (1, 3, 2):
            y_arrival(w, zz, d).wait_recv()
        c_copy(w, zz).start()

    stage_a(0, 0)
    for d in (1, 3):
        q_copy(d).start()

    def send_z(w):
        def step(d, carry):
            z_copy(w, d).start()
            return carry
        lax.fori_loop(1, NZ - z, step, 0)

    send_z(0)
    q_copy(2).start()
    send_z(1)

    lane = lax.broadcasted_iota(jnp.int32, (8, 128), 1)
    sub = lax.broadcasted_iota(jnp.int32, (8, 128), 0)
    pick = 8 * (lane // 64) + 2 * x + (lane // 32) % 2
    for n in range(NZ * TILE // 128):
        bits = bm[:, (n // 8) * 128:(n // 8 + 1) * 128]
        here = jnp.take_along_axis(bits, pick + 16 * (n % 8), axis=1)
        column = 16 * n + pick
        token = 256 * (2 * n + lane // 64) + 64 * x + lane % 64
        cp[:, n * 128:(n + 1) * 128] = jnp.where((here == 1) | (column == 8 * gr + sub), token, BIG)

    scale = math.log2(math.e) / math.sqrt(HEAD_DIM)
    lane64 = lax.broadcasted_iota(jnp.int32, (TOK, 128), 1)
    sub64 = lax.broadcasted_iota(jnp.int32, (TOK, 128), 0)
    eye = lane64 == sub64

    def prepare_q(j):
        for h in range(HEADS):
            hi, lo = split(qbuf[j, :, h * HEAD_DIM:(h + 1) * HEAD_DIM] * scale)
            for i, part in enumerate((hi, lo, hi, lo)):
                qcat[j, h * TOK:(h + 1) * TOK, i * 128:(i + 1) * 128] = part
        mx[j] = jnp.full((PAIRS, 128), NEG, F32)

    def prepare_k(zz):
        hi, lo = split(kvbuf[0, zz].reshape(TILE, HEAD_DIM))
        rows = pl.ds(pl.multiple_of(zz * TILE, TILE), TILE)
        for i, part in enumerate((hi, hi, lo, lo)):
            kcat[rows, i * 128:(i + 1) * 128] = part

    def prepare_v(zz):
        hi, lo = split(kvbuf[1, zz].reshape(TILE, HEAD_DIM))
        rows = pl.ds(pl.multiple_of(zz * TILE, TILE), TILE)
        vcat[rows, :128] = hi
        vcat[rows, 128:] = lo

    def scores(j, zz):
        length_row = lens[pl.ds(2 * y + j // 2, 1), :]
        length = jnp.max(
            jnp.where(lane64 == sub64 + 64 * (j % 2), jnp.broadcast_to(length_row, (TOK, 128)), 0), axis=1, keepdims=True)
        row = 256 * gr + 64 * j + lax.broadcasted_iota(jnp.int32, (TOK, KT), 0)
        low = row - length
        for n in range(TILE // KT):
            off = pl.multiple_of(zz * TILE + n * KT, KT)
            sc = lax.dot_general(
                qcat[j], kcat[pl.ds(off, KT), :], (((1,), (1,)), ((), ())), preferred_element_type=F32)
            tokens = jnp.concatenate(
                [jnp.broadcast_to(cp[pl.ds(2 * j + i, 1), pl.ds(off, KT)], (32, KT)) for i in range(2)], axis=0)
            ok = (tokens <= row) & (tokens > low)
            sc = jnp.where(ok[None], sc.reshape(HEADS, TOK, KT), NEG).reshape(PAIRS, KT)
            s[j, :, pl.ds(off, KT)] = sc
            m = mx[j]
            for a in range(KT // 128):
                m = jnp.maximum(m, sc[:, a * 128:(a + 1) * 128])
            mx[j] = m

    prepare_q(x)

    stage_b(0, 0)

    @pl.when(z >= 1)
    def _():
        stage_a(0, 1)

    def own_step(i, carry):
        @pl.when(i + 2 <= z)
        def _():
            stage_a(0, i + 2)

        @pl.when(i + 1 <= z)
        def _():
            stage_b(0, i + 1)
        c_arrival(0, z - i).wait_recv()
        prepare_k(z - i)
        scores(x, z - i)
        return carry

    lax.fori_loop(0, z + 1, own_step, 0)

    for turn, d in enumerate((1, 3, 2)):
        q_arrival(d).wait_recv()
        j = lax.rem(x + d, NX)
        prepare_q(j)

        def other_step(i, carry, turn=turn, j=j):
            if turn == 0:
                stage_a(1, i)
            elif turn == 1:
                stage_b(1, i)
            else:
                c_arrival(1, z - i).wait_recv()
                prepare_v(z - i)
            scores(j, z - i)
            return carry

        lax.fori_loop(0, z + 1, other_step, 0)

    def attend(j, write):
        m = jnp.maximum(jnp.max(mx[j], axis=1, keepdims=True), FLOOR)
        mx[j] = jnp.broadcast_to(m, (PAIRS, 128))
        acc[...] = jnp.zeros_like(acc)
        lacc[...] = jnp.zeros_like(lacc)

        def part(off, width):
            shift = jnp.concatenate([mx[j]] * (width // 128), axis=1)
            p = jnp.exp2(s[j, :, pl.ds(off, width)] - shift)
            hi, lo = split(p)
            v = vcat[pl.ds(off, width), :]
            acc[...] += jnp.dot(hi, v, preferred_element_type=F32) + jnp.dot(lo, v, preferred_element_type=F32)
            total = p[:, :128]
            for a in range(1, width // 128):
                total = total + p[:, a * 128:(a + 1) * 128]
            lacc[...] += total

        def pair_step(i, carry):
            part(pl.multiple_of(i * 2 * TILE, 2 * TILE), 2 * TILE)
            return carry

        lax.fori_loop(0, (z + 1) // 2, pair_step, 0)

        @pl.when(z % 2 == 0)
        def _():
            part(pl.multiple_of(z * TILE, TILE), TILE)

        total = jnp.sum(lacc[...], axis=1, keepdims=True)
        some = total > 0
        inverse = jnp.where(some, 1.0 / jnp.where(some, total, 1.0), 0.0)
        lse = jnp.where(some, m + jnp.log2(jnp.where(some, total, 1.0)), NEG)
        write((acc[:, :128] + acc[:, 128:]) * inverse, lse)

    def to_lanes(lse):
        spread = jnp.broadcast_to(lse, (PAIRS, 128)).reshape(HEADS, TOK, 128)
        return jnp.sum(jnp.where(eye[None], spread, 0.0), axis=1)

    for d in (1, 3, 2):
        def write(value, lse, d=d):
            osend[d - 1] = value
            lsend[d - 1] = to_lanes(lse)
            o_copy(d).start()
            l_copy(d).start()
        attend(lax.rem(x + d, NX), write)

    def write_own(value, lse):
        own[...] = value
        lsend[3] = to_lanes(lse)
    attend(x, write_own)

    for d in (1, 3, 2):
        o_copy(d).wait_recv()
        l_copy(d).wait_recv()
    parts = [lsend[3], lrecv[0], lrecv[1], lrecv[2]]
    top = functools.reduce(jnp.maximum, parts)
    weights = [jnp.exp2(part - top) for part in parts]
    total = weights[0] + weights[1] + weights[2] + weights[3]
    ln_ref[...] = ((top + jnp.log2(total)) * math.log(2.0))[:, :TOK]
    shares = [weight / total for weight in weights]
    for h in range(HEADS):
        rows = slice(h * TOK, (h + 1) * TOK)
        blocks = [own[rows, :], orecv[0, rows, :], orecv[1, rows, :], orecv[2, rows, :]]
        result = jnp.zeros((TOK, 128), F32)
        for share, block in zip(shares, blocks):
            column = jnp.sum(jnp.where(eye, jnp.broadcast_to(share[h:h + 1, :], (TOK, 128)), 0.0), axis=1, keepdims=True)
            result = result + column * block
        out_ref[:, h * HEAD_DIM:(h + 1) * HEAD_DIM] = result

    for d in (1, 2, 3):
        q_copy(d).wait_send()
        o_copy(d).wait_send()
        l_copy(d).wait_send()

    def drain_z(d, carry):
        z_copy(0, d).wait_send()
        z_copy(1, d).wait_send()
        return carry

    lax.fori_loop(1, NZ - z, drain_z, 0)

    def drain(i, carry):
        for w in range(2):
            for d in (1, 2, 3):
                y_copy(w, z - i, d).wait_send()
            c_copy(w, z - i).wait_send()
        return carry

    lax.fori_loop(0, z + 1, drain, 0)


def shards(queries, keys, values, block_mask, key_lengths):
    lengths = key_lengths.reshape(128, 128)
    dma = pltpu.SemaphoreType.DMA
    anywhere = pl.BlockSpec(memory_space=pl.ANY)
    vmem = pl.BlockSpec(memory_space=pltpu.VMEM)
    return pl.pallas_call(
        kernel,
        out_shape=(
            jax.ShapeDtypeStruct((TOK, HEADS * HEAD_DIM), F32),
            jax.ShapeDtypeStruct((HEADS, TOK), F32),
        ),
        in_specs=[anywhere] * 5,
        out_specs=(vmem, vmem),
        scratch_shapes=[
            pltpu.VMEM((NX, TOK, HEADS * HEAD_DIM), F32),
            pltpu.VMEM((NX, PAIRS, 512), BF16),
            pltpu.VMEM((2, NZ, 2, NY, TOK, HEAD_DIM), F32),
            pltpu.VMEM((NZ * TILE, 512), BF16),
            pltpu.VMEM((NZ * TILE, 256), BF16),
            pltpu.VMEM((NX, PAIRS, NZ * TILE), F32),
            pltpu.VMEM((NX, PAIRS, 128), F32),
            pltpu.VMEM((PAIRS, 256), F32),
            pltpu.VMEM((PAIRS, 128), F32),
            pltpu.VMEM((3, PAIRS, 128), F32),
            pltpu.VMEM((4, HEADS, 128), F32),
            pltpu.VMEM((3, PAIRS, 128), F32),
            pltpu.VMEM((3, HEADS, 128), F32),
            pltpu.VMEM((PAIRS, 128), F32),
            pltpu.VMEM((8, 512), jnp.int32),
            pltpu.VMEM((8, 128), jnp.int32),
            pltpu.VMEM((8, NZ * TILE), jnp.int32),
            dma((5,)),
            dma((NX,)), dma((NX,)),
            dma((2, NZ)), dma((2, NZ)),
            dma((2, NZ, NY)), dma((2, NZ, NY)),
            dma((2, NZ)), dma((2, NZ)),
            dma((4,)), dma((4,)), dma((4,)), dma((4,)),
        ],
        compiler_params=pltpu.CompilerParams(
            vmem_limit_bytes=60 * 2**20, collective_id=0, has_side_effects=True),
        cost_estimate=pl.CostEstimate(flops=8 * 2 * 128 * 2**22, bytes_accessed=2**22, transcendentals=2**22),
    )(queries, keys, values, block_mask, lengths)


def solution(mesh):
    in_specs = (P(("qb", "kb"), None), P(("qb", "kb"), None), P(("qb", "kb"), None), P(), P())
    out_specs = (P(("qb", "kb"), None), P(None, ("qb", "kb")))
    return jax.shard_map(shards, mesh=mesh, in_specs=in_specs, out_specs=out_specs, check_vma=False)
```

time: 472 us -> 73.5 us (0.16)
  the two profiles are of different devices: /device:TPU:224 before, /device:TPU:226 now
where the time goes in v1:
time: 73.5 us; the launch traced here: 73.4 us
  Pallas kernels  70.5 us (96%)
  local copies, waits for them, and re-layouts  2.27 us (3%)
    pallas_call x1, Pallas kernels, shards(): pl.pallas_call(kernel, out_shape=(jax.ShapeDtypeStruct((TOK, HEADS * HEAD...  70.5 us
    unnamed x4, local copies, waits for them, and re-layouts  2.27 us

profile of v1, /device:TPU:226, one launch (start us, length us, event | category | flops | bytes accessed | tf_op | source)
XLA Modules:
  0.0 73.4 jit_solution(6808813009860483769)
XLA Ops:
  0.6 70.5 %shard_map.68 = (f32[64,1024]{1,0:T(8,128)}, f32[8,64]{1,0:T(8,128)}) custom-call(f32[64,1024]{1,0:T(8,128)} %q_ref.1, f32[64,128]{1,0:T(8,128)} %k_ref.1, f32[64,128]{1,0:T(8,128)} %v_ref.1, s32[512,512]{1,0:T(8,128)} %bm_ref.1, s32[128,128]{1,0:T(8,128)} %bitcast.1), custom_call_target="tpu_custom_call" | custom-call | flops 8589934592 | bytes 4194304 | tf_op jit(solution)/shard_map/pallas_call | solution.py:342
  71.1 0.0 copy-start
  71.1 1.7 %copy.9 = f32[64,1024]{1,0:T(8,128)} copy(f32[64,1024]{1,0:T(8,128)} %get-tuple-element.4) | data formatting | bytes 524288
  72.8 0.0 copy-done
  72.8 0.6 copy.10
Async XLA Ops:
  71.1 1.7 %copy-start = (f32[8,64]{1,0:T(8,128)S(1)}, f32[8,64]{1,0:T(8,128)}, u32[]{:S(2)}) copy-start(f32[8,64]{1,0:T(8,128)} %get-tuple-element.5) | copy-start | bytes 6148

commit v2 on v1

v2 whole, which is shorter than its diff:
```python
import functools
import math

import jax
import jax.numpy as jnp
from jax import lax
from jax.experimental import pallas as pl
from jax.experimental.pallas import tpu as pltpu
from jax.sharding import PartitionSpec as P

HEADS = 8
HEAD_DIM = 128
TOK = 64
PAIRS = HEADS * TOK
NX, NY, NZ = 4, 4, 8
TILE = 2 * NY * TOK
NEG = -1e30
FLOOR = -1e29
BIG = 1 << 30
MESH = pl.DeviceIdType.MESH
F32 = jnp.float32
BF16 = jnp.bfloat16
STEP = 2 * TILE
DELTAS = (0, 1, 3, 2)
AHEAD_A, AHEAD_B, AHEAD_C = 10, 6, 2


def split(x):
    hi = x.astype(BF16)
    lo = (x - hi.astype(F32)).astype(BF16)
    return hi, lo


def kernel(
    q_ref, k_ref, v_ref, bm_ref, kl_ref, out_ref, ln_ref,
    qbuf, qcat, kvbuf, kcat, vcat, s, mx, acc, lacc, osend, lsend, orecv, lrecv, own, bm, lens, low, cp,
    local_sem, qs, qr, zs, zr, ys, yr, hs, hr, cs, cr, os_, or_, ls_, lr_,
):
    qb = lax.axis_index("qb")
    kb = lax.axis_index("kb")
    z, c = lax.div(qb, 2), lax.rem(qb, 2)
    y, x = lax.div(kb, NX), lax.rem(kb, NX)
    gr = qb * NY + y
    last = 2 * z + 1
    partner = (qb + 1 - 2 * c, kb)

    def at_x(d):
        return (qb, y * NX + lax.rem(x + d, NX))

    def at_y(d):
        return (qb, lax.rem(y + d, NY) * NX + x)

    def at_z(d):
        return (lax.rem(qb + 2 * d, 2 * NZ), kb)

    loads = [
        pltpu.make_async_copy(k_ref, kvbuf.at[0, z, c, y], local_sem.at[0]),
        pltpu.make_async_copy(v_ref, kvbuf.at[1, z, c, y], local_sem.at[1]),
        pltpu.make_async_copy(q_ref, qbuf.at[x], local_sem.at[2]),
        pltpu.make_async_copy(bm_ref.at[pl.ds(pl.multiple_of(gr * 8, 8), 8)], bm, local_sem.at[3]),
        pltpu.make_async_copy(kl_ref.at[pl.ds(pl.multiple_of(qb * 8, 8), 8)], lens, local_sem.at[4]),
    ]
    for copy in loads:
        copy.start()

    barrier = pltpu.get_barrier_semaphore()
    peers = [at_x(d) for d in (1, 2, 3)] + [at_y(d) for d in (1, 3)] + [at_z(d) for d in range(1, NZ)] + [partner]
    for peer in peers:
        pl.semaphore_signal(barrier, inc=1, device_id=peer, device_id_type=MESH)
    for copy in loads:
        copy.wait()
    pl.semaphore_wait(barrier, len(peers))

    def remote(ref, send_sem, recv_sem, device, dst=None):
        return pltpu.make_async_remote_copy(
            src_ref=ref, dst_ref=ref if dst is None else dst, send_sem=send_sem, recv_sem=recv_sem,
            device_id=device, device_id_type=MESH)

    def q_copy(d):
        return remote(qbuf.at[x], qs.at[d], qr.at[x], at_x(d))

    def q_arrival(d):
        src = lax.rem(x + d, NX)
        return remote(qbuf.at[src], qs.at[0], qr.at[src], at_x(d))

    def z_copy(w, d):
        return remote(kvbuf.at[w, z, c, y], zs.at[w, d], zr.at[w, z], at_z(d))

    def z_arrival(w, zz):
        return remote(kvbuf.at[w, zz, c, y], zs.at[w, 0], zr.at[w, zz], at_z(1))

    def y_copy(w, zz, d):
        return remote(kvbuf.at[w, zz, c, y], ys.at[w, zz, d], yr.at[w, zz, y], at_y(d))

    def y_arrival(w, zz, d):
        src = lax.rem(y + d, NY)
        return remote(kvbuf.at[w, zz, c, src], ys.at[w, zz, 0], yr.at[w, zz, src], at_y(d))

    def half_copy(w, zz, n):
        src = lax.rem(y + (3, 1)[n], NY)
        return remote(kvbuf.at[w, zz, c, src, pl.ds(n * 32, 32)], hs.at[w, zz, n], hr.at[w, zz, n], at_y((1, 3)[n]))

    def half_arrival(w, zz, n):
        src = lax.rem(y + 2, NY)
        return remote(kvbuf.at[w, zz, c, src, pl.ds(n * 32, 32)], hs.at[w, zz, n], hr.at[w, zz, n], at_y(1))

    def c_copy(w, zz):
        return remote(kvbuf.at[w, zz, c], cs.at[w, zz], cr.at[w, zz], partner)

    def c_arrival(w, zz):
        return remote(kvbuf.at[w, zz, 1 - c], cs.at[w, zz], cr.at[w, zz], partner)

    def o_copy(d):
        return remote(osend.at[d - 1], os_.at[d], or_.at[d], at_x(d), orecv.at[d - 1])

    def l_copy(d):
        return remote(lsend.at[d - 1], ls_.at[d], lr_.at[d], at_x(d), lrecv.at[d - 1])

    def place(u):
        w = (u > z).astype(jnp.int32)
        return w, z - u + w * (z + 1)

    def stage_a(u):
        w, zz = place(u)

        @pl.when(zz != z)
        def _():
            z_arrival(w, zz).wait_recv()
        for d in (1, 3):
            y_copy(w, zz, d).start()

    def stage_b(u):
        w, zz = place(u)
        for n, d in ((0, 3), (1, 1)):
            y_arrival(w, zz, d).wait_recv()
            half_copy(w, zz, n).start()

    def stage_c(u):
        w, zz = place(u)
        for n in range(2):
            half_arrival(w, zz, n).wait_recv()
        c_copy(w, zz).start()

    def advance(u):
        for stage, ahead in ((stage_c, AHEAD_C), (stage_b, AHEAD_B), (stage_a, AHEAD_A)):
            step = u + ahead

            @pl.when((step >= 0) & (step <= last))
            def _(stage=stage, step=step):
                stage(step)

    stage_a(0)
    for d in (1, 3):
        q_copy(d).start()

    def send_z(w):
        def step(d, carry):
            z_copy(w, d).start()
            return carry
        lax.fori_loop(1, NZ - z, step, 0)

    send_z(0)
    q_copy(2).start()
    send_z(1)

    lane = lax.broadcasted_iota(jnp.int32, (8, 128), 1)
    sub = lax.broadcasted_iota(jnp.int32, (8, 128), 0)
    pick = 8 * (lane // 64) + 2 * x + (lane // 32) % 2
    for n in range(NZ * TILE // 128):
        bits = bm[:, (n // 8) * 128:(n // 8 + 1) * 128]
        here = jnp.take_along_axis(bits, pick + 16 * (n % 8), axis=1)
        column = 16 * n + pick
        token = 256 * (2 * n + lane // 64) + 64 * x + lane % 64
        cp[:, n * 128:(n + 1) * 128] = jnp.where((here == 1) | (column == 8 * gr + sub), token, BIG)

    scale = math.log2(math.e) / math.sqrt(HEAD_DIM)
    lane64 = lax.broadcasted_iota(jnp.int32, (TOK, 128), 1)
    sub64 = lax.broadcasted_iota(jnp.int32, (TOK, 128), 0)
    eye = lane64 == sub64

    def block_of(slot):
        return lax.rem(x + DELTAS[slot], NX)

    for slot in range(NX):
        j = block_of(slot)
        length_row = lens[pl.ds(2 * y + j // 2, 1), :]
        length = jnp.max(
            jnp.where(lane64 == sub64 + 64 * (j % 2), jnp.broadcast_to(length_row, (TOK, 128)), 0), axis=1, keepdims=True)
        low[slot] = 256 * gr + 64 * j + sub64 - length

    mx[...] = jnp.full(mx.shape, NEG, F32)

    def prepare_q(slot):
        j = block_of(slot)
        for h in range(HEADS):
            rows = slice(slot * PAIRS + h * TOK, slot * PAIRS + (h + 1) * TOK)
            hi, lo = split(qbuf[j, :, h * HEAD_DIM:(h + 1) * HEAD_DIM] * scale)
            for i, part in enumerate((hi, lo, hi, lo)):
                qcat[rows, i * 128:(i + 1) * 128] = part

    def prepare_k(zz):
        hi, lo = split(kvbuf[0, zz].reshape(TILE, HEAD_DIM))
        rows = pl.ds(pl.multiple_of(zz * TILE, TILE), TILE)
        for i, part in enumerate((hi, hi, lo, lo)):
            kcat[rows, i * 128:(i + 1) * 128] = part

    def prepare_v(zz):
        hi, lo = split(kvbuf[1, zz].reshape(TILE, HEAD_DIM))
        rows = pl.ds(pl.multiple_of(zz * TILE, TILE), TILE)
        vcat[rows, :128] = hi
        vcat[rows, 128:] = lo

    def scores(first, count, zz):
        keys = pl.ds(pl.multiple_of(zz * TILE, TILE), TILE)
        raw = lax.dot_general(
            qcat[first * PAIRS:(first + count) * PAIRS, :], kcat[keys, :], (((1,), (1,)), ((), ())),
            preferred_element_type=F32)
        for n in range(count):
            slot = first + n
            j = block_of(slot)
            rows = slice(slot * PAIRS, (slot + 1) * PAIRS)
            tokens = jnp.concatenate(
                [jnp.broadcast_to(cp[pl.ds(2 * j + i, 1), keys], (32, TILE)) for i in range(2)], axis=0)
            row = 256 * gr + 64 * j + lax.broadcasted_iota(jnp.int32, (TOK, TILE), 0)
            ok = (tokens <= row) & (tokens > jnp.concatenate([low[slot]] * (TILE // 128), axis=1))
            sc = raw[n * PAIRS:(n + 1) * PAIRS].reshape(HEADS, TOK, TILE)
            sc = jnp.where(ok[None], sc, NEG).reshape(PAIRS, TILE)
            s[rows, keys] = sc
            m = mx[rows, :]
            for a in range(TILE // 128):
                m = jnp.maximum(m, sc[:, a * 128:(a + 1) * 128])
            mx[rows, :] = m

    prepare_q(0)

    def warm(u, carry):
        advance(u)
        return carry

    lax.fori_loop(1 - AHEAD_A, 0, warm, 0)
    planes = z + 1

    for slot in (1, 2):
        q_arrival(DELTAS[slot]).wait_recv()
        prepare_q(slot)

    def near_step(u, carry):
        advance(u)
        c_arrival(0, z - u).wait_recv()
        prepare_k(z - u)
        scores(1, 2, z - u)
        return carry

    lax.fori_loop(0, planes, near_step, 0)

    q_arrival(DELTAS[3]).wait_recv()
    prepare_q(3)

    def slot_rows(slot):
        return pl.ds(pl.multiple_of(slot * PAIRS, PAIRS), PAIRS)

    def settle_max(slot, carry):
        rows = slot_rows(slot)
        m = jnp.maximum(jnp.max(mx[rows, :], axis=1, keepdims=True), FLOOR)
        mx[rows, :] = jnp.broadcast_to(m, (PAIRS, 128))
        return carry

    acc[...] = jnp.zeros_like(acc)
    lacc[...] = jnp.zeros_like(lacc)

    def weigh(slot, start, width):
        rows = slot_rows(slot)
        keys = pl.ds(pl.multiple_of(start * TILE, TILE), width)
        shift = jnp.concatenate([mx[rows, :]] * (width // 128), axis=1)
        p = jnp.exp2(s[rows, keys] - shift)
        hi, lo = split(p)
        v = vcat[keys, :]
        acc[rows, :] += jnp.dot(hi, v, preferred_element_type=F32) + jnp.dot(lo, v, preferred_element_type=F32)
        total = p[:, :128]
        for a in range(1, width // 128):
            total = total + p[:, a * 128:(a + 1) * 128]
        lacc[rows, :] += total

    def weigh_pair(slot, g):
        weigh(slot, z - 2 * g - 1, STEP)

    pairs = planes // 2

    early = ((3, 3, 0), (4, 3, 1), (5, 2, 0), (6, 3, 2), (7, 2, 1))

    def value_step(k, carry):
        advance(planes + k)
        for n in range(3):
            @pl.when(3 * k + n < planes)
            def _(n=n):
                scores(3, 1, z - 3 * k - n)

        @pl.when(k == jnp.minimum(z, 2))
        def _():
            lax.fori_loop(1, NX, settle_max, 0)
        @pl.when(k >= 3)
        def _():
            second = (k == 5) | (k == 7)
            weigh_pair(jnp.where(second, 2, 3), jnp.where(k == 6, 2, jnp.where((k == 4) | (k == 7), 1, 0)))
        c_arrival(1, z - k).wait_recv()
        prepare_v(z - k)
        return carry

    lax.fori_loop(0, planes, value_step, 0)

    def to_lanes(lse):
        spread = jnp.broadcast_to(lse, (PAIRS, 128)).reshape(HEADS, TOK, 128)
        return jnp.sum(jnp.where(eye[None], spread, 0.0), axis=1)

    def attend(slot, done):
        def pair_step(g, carry):
            weigh_pair(slot, g)
            return carry

        lax.fori_loop(done, pairs, pair_step, 0)

        @pl.when(planes % 2 == 1)
        def _():
            weigh(slot, 0, TILE)
        rows = slice(slot * PAIRS, (slot + 1) * PAIRS)
        total = jnp.sum(lacc[rows, :], axis=1, keepdims=True)
        some = total > 0
        inverse = jnp.where(some, 1.0 / jnp.where(some, total, 1.0), 0.0)
        lse = jnp.where(some, mx[rows, :] + jnp.log2(jnp.where(some, total, 1.0)), NEG)
        return (acc[rows, :128] + acc[rows, 128:]) * inverse, to_lanes(lse)

    for slot in (3, 2, 1):
        d = DELTAS[slot]
        done = jnp.int32(0)
        for k, of, _ in early:
            if of == slot:
                done += (planes > k).astype(jnp.int32)
        value, lse = attend(slot, done)
        lsend[d - 1] = lse
        l_copy(d).start()
        osend[d - 1] = value
        o_copy(d).start()

    def own_step(u, carry):
        scores(0, 1, z - u)
        return carry

    lax.fori_loop(0, planes, own_step, 0)
    settle_max(0, 0)
    value, lse = attend(0, 0)
    own[...] = value
    lsend[3] = lse

    for d in (1, 3, 2):
        l_copy(d).wait_recv()
    parts = [lsend[3], lrecv[0], lrecv[1], lrecv[2]]
    top = functools.reduce(jnp.maximum, parts)
    weights = [jnp.exp2(part - top) for part in parts]
    total = weights[0] + weights[1] + weights[2] + weights[3]
    ln_ref[...] = ((top + jnp.log2(total)) * math.log(2.0))[:, :TOK]
    shares = [weight / total for weight in weights]

    def column(share, h):
        return jnp.sum(jnp.where(eye, jnp.broadcast_to(share[h:h + 1, :], (TOK, 128)), 0.0), axis=1, keepdims=True)

    for h in range(HEADS):
        rows = slice(h * TOK, (h + 1) * TOK)
        out_ref[:, h * HEAD_DIM:(h + 1) * HEAD_DIM] = own[rows, :] * column(shares[0], h)
    for d in (2, 3, 1):
        o_copy(d).wait_recv()
        for h in range(HEADS):
            rows = slice(h * TOK, (h + 1) * TOK)
            out_ref[:, h * HEAD_DIM:(h + 1) * HEAD_DIM] += orecv[d - 1, rows, :] * column(shares[d], h)

    for d in (1, 2, 3):
        q_copy(d).wait_send()
        o_copy(d).wait_send()
        l_copy(d).wait_send()

    def drain_z(d, carry):
        z_copy(0, d).wait_send()
        z_copy(1, d).wait_send()
        return carry

    lax.fori_loop(1, NZ - z, drain_z, 0)

    def drain(u, carry):
        w, zz = place(u)
        for d in (1, 3):
            y_copy(w, zz, d).wait_send()
        for n in range(2):
            half_copy(w, zz, n).wait_send()
        c_copy(w, zz).wait_send()
        return carry

    lax.fori_loop(0, last + 1, drain, 0)


def shards(queries, keys, values, block_mask, key_lengths):
    lengths = key_lengths.reshape(128, 128)
    dma = pltpu.SemaphoreType.DMA
    anywhere = pl.BlockSpec(memory_space=pl.ANY)
    vmem = pl.BlockSpec(memory_space=pltpu.VMEM)
    return pl.pallas_call(
        kernel,
        out_shape=(
            jax.ShapeDtypeStruct((TOK, HEADS * HEAD_DIM), F32),
            jax.ShapeDtypeStruct((HEADS, TOK), F32),
        ),
        in_specs=[anywhere] * 5,
        out_specs=(vmem, vmem),
        scratch_shapes=[
            pltpu.VMEM((NX, TOK, HEADS * HEAD_DIM), F32),
            pltpu.VMEM((NX * PAIRS, 512), BF16),
            pltpu.VMEM((2, NZ, 2, NY, TOK, HEAD_DIM), F32),
            pltpu.VMEM((NZ * TILE, 512), BF16),
            pltpu.VMEM((NZ * TILE, 256), BF16),
            pltpu.VMEM((NX * PAIRS, NZ * TILE), F32),
            pltpu.VMEM((NX * PAIRS, 128), F32),
            pltpu.VMEM((NX * PAIRS, 256), F32),
            pltpu.VMEM((NX * PAIRS, 128), F32),
            pltpu.VMEM((3, PAIRS, 128), F32),
            pltpu.VMEM((4, HEADS, 128), F32),
            pltpu.VMEM((3, PAIRS, 128), F32),
            pltpu.VMEM((3, HEADS, 128), F32),
            pltpu.VMEM((PAIRS, 128), F32),
            pltpu.VMEM((8, 512), jnp.int32),
            pltpu.VMEM((8, 128), jnp.int32),
            pltpu.VMEM((NX, TOK, 128), jnp.int32),
            pltpu.VMEM((8, NZ * TILE), jnp.int32),
            dma((5,)),
            dma((NX,)), dma((NX,)),
            dma((2, NZ)), dma((2, NZ)),
            dma((2, NZ, NY)), dma((2, NZ, NY)),
            dma((2, NZ, 2)), dma((2, NZ, 2)),
            dma((2, NZ)), dma((2, NZ)),
            dma((4,)), dma((4,)), dma((4,)), dma((4,)),
        ],
        compiler_params=pltpu.CompilerParams(
            vmem_limit_bytes=60 * 2**20, collective_id=0, has_side_effects=True),
        cost_estimate=pl.CostEstimate(flops=8 * 2 * 128 * 2**22, bytes_accessed=2**22, transcendentals=2**22),
    )(queries, keys, values, block_mask, lengths)


def solution(mesh):
    in_specs = (P(("qb", "kb"), None), P(("qb", "kb"), None), P(("qb", "kb"), None), P(), P())
    out_specs = (P(("qb", "kb"), None), P(None, ("qb", "kb")))
    return jax.shard_map(shards, mesh=mesh, in_specs=in_specs, out_specs=out_specs, check_vma=False)
```

time: 73.5 us -> 58.3 us (0.79)
  the two profiles are of different devices: /device:TPU:226 before, /device:TPU:224 now
where the time goes in v2:
time: 58.3 us; the launch traced here: 57.7 us
  Pallas kernels  54.7 us (94%)
  local copies, waits for them, and re-layouts  2.27 us (4%)
  between operations  0.65 us (1%)
    pallas_call x1, Pallas kernels, shards(): pl.pallas_call(kernel, out_shape=(jax.ShapeDtypeStruct((TOK, HEADS * HEAD...  54.7 us
    unnamed x4, local copies, waits for them, and re-layouts  2.27 us

profile of v2, /device:TPU:224, one launch (start us, length us, event | category | flops | bytes accessed | tf_op | source)
XLA Modules:
  0.0 57.7 jit_solution(1046468466210465919)
XLA Ops:
  0.6 54.7 %shard_map.68 = (f32[64,1024]{1,0:T(8,128)}, f32[8,64]{1,0:T(8,128)}) custom-call(f32[64,1024]{1,0:T(8,128)} %q_ref.1, f32[64,128]{1,0:T(8,128)} %k_ref.1, f32[64,128]{1,0:T(8,128)} %v_ref.1, s32[512,512]{1,0:T(8,128)} %bm_ref.1, s32[128,128]{1,0:T(8,128)} %bitcast.1), custom_call_target="tpu_custom_call" | custom-call | flops 8589934592 | bytes 4194304 | tf_op jit(solution)/shard_map/pallas_call | solution.py:404
  55.4 0.0 copy-start
  55.4 1.7 %copy.9 = f32[64,1024]{1,0:T(8,128)} copy(f32[64,1024]{1,0:T(8,128)} %get-tuple-element.4) | data formatting | bytes 524288
  57.1 0.0 copy-done
  57.1 0.6 %copy.10 = f32[8,64]{1,0:T(8,128)} copy(f32[8,64]{1,0:T(8,128)S(1)} %copy-done) | data formatting | bytes 4096
Async XLA Ops:
  55.4 1.7 %copy-start = (f32[8,64]{1,0:T(8,128)S(1)}, f32[8,64]{1,0:T(8,128)}, u32[]{:S(2)}) copy-start(f32[8,64]{1,0:T(8,128)} %get-tuple-element.5) | copy-start | bytes 6148

commit v3 on v2

--- a/solution.py
+++ b/solution.py
@@ -22,7 +22,7 @@
 BF16 = jnp.bfloat16
 STEP = 2 * TILE
 DELTAS = (0, 1, 3, 2)
-AHEAD_A, AHEAD_B, AHEAD_C = 10, 6, 2
+AHEAD_A, AHEAD_C = 7, 2
 
 
 def split(x):
@@ -34,7 +34,7 @@
 def kernel(
     q_ref, k_ref, v_ref, bm_ref, kl_ref, out_ref, ln_ref,
     qbuf, qcat, kvbuf, kcat, vcat, s, mx, acc, lacc, osend, lsend, orecv, lrecv, own, bm, lens, low, cp,
-    local_sem, qs, qr, zs, zr, ys, yr, hs, hr, cs, cr, os_, or_, ls_, lr_,
+    local_sem, qs, qr, zs, zr, zf, ys, yr, cs, cr, os_, or_, ls_, lr_,
 ):
     qb = lax.axis_index("qb")
     kb = lax.axis_index("kb")
@@ -64,7 +64,7 @@
         copy.start()
 
     barrier = pltpu.get_barrier_semaphore()
-    peers = [at_x(d) for d in (1, 2, 3)] + [at_y(d) for d in (1, 3)] + [at_z(d) for d in range(1, NZ)] + [partner]
+    peers = [at_x(d) for d in (1, 2, 3)] + [at_y(d) for d in (1, 2, 3)] + [at_z(d) for d in range(1, NZ)] + [partner]
     for peer in peers:
         pl.semaphore_signal(barrier, inc=1, device_id=peer, device_id_type=MESH)
     for copy in loads:
@@ -86,6 +86,12 @@
     def z_copy(w, d):
         return remote(kvbuf.at[w, z, c, y], zs.at[w, d], zr.at[w, z], at_z(d))
 
+    def straight(d):
+        return (d < 3) | (d > 4) | (z + d == NZ - 1)
+
+    def forward(w, e):
+        return remote(kvbuf.at[w, z - 2, c, y], zf.at[w, e], zr.at[w, z - 2], at_z(e))
+
     def z_arrival(w, zz):
         return remote(kvbuf.at[w, zz, c, y], zs.at[w, 0], zr.at[w, zz], at_z(1))
 
@@ -96,14 +102,6 @@
         src = lax.rem(y + d, NY)
         return remote(kvbuf.at[w, zz, c, src], ys.at[w, zz, 0], yr.at[w, zz, src], at_y(d))
 
-    def half_copy(w, zz, n):
-        src = lax.rem(y + (3, 1)[n], NY)
-        return remote(kvbuf.at[w, zz, c, src, pl.ds(n * 32, 32)], hs.at[w, zz, n], hr.at[w, zz, n], at_y((1, 3)[n]))
-
-    def half_arrival(w, zz, n):
-        src = lax.rem(y + 2, NY)
-        return remote(kvbuf.at[w, zz, c, src, pl.ds(n * 32, 32)], hs.at[w, zz, n], hr.at[w, zz, n], at_y(1))
-
     def c_copy(w, zz):
         return remote(kvbuf.at[w, zz, c], cs.at[w, zz], cr.at[w, zz], partner)
 
@@ -126,23 +124,21 @@
         @pl.when(zz != z)
         def _():
             z_arrival(w, zz).wait_recv()
-        for d in (1, 3):
+        for e in (1, 2):
+            @pl.when((zz == z - 2) & (z + e < NZ - 1))
+            def _(e=e):
+                forward(w, e).start()
+        for d in (2, 1, 3):
             y_copy(w, zz, d).start()
-
-    def stage_b(u):
-        w, zz = place(u)
-        for n, d in ((0, 3), (1, 1)):
-            y_arrival(w, zz, d).wait_recv()
-            half_copy(w, zz, n).start()
 
     def stage_c(u):
         w, zz = place(u)
-        for n in range(2):
-            half_arrival(w, zz, n).wait_recv()
+        for d in (1, 3, 2):
+            y_arrival(w, zz, d).wait_recv()
         c_copy(w, zz).start()
 
     def advance(u):
-        for stage, ahead in ((stage_c, AHEAD_C), (stage_b, AHEAD_B), (stage_a, AHEAD_A)):
+        for stage, ahead in ((stage_c, AHEAD_C), (stage_a, AHEAD_A)):
             step = u + ahead
 
             @pl.when((step >= 0) & (step <= last))
@@ -155,7 +151,9 @@
 
     def send_z(w):
         def step(d, carry):
-            z_copy(w, d).start()
+            @pl.when(straight(d))
+            def _():
+                z_copy(w, d).start()
             return carry
         lax.fori_loop(1, NZ - z, step, 0)
 
@@ -378,18 +376,24 @@
         l_copy(d).wait_send()
 
     def drain_z(d, carry):
-        z_copy(0, d).wait_send()
-        z_copy(1, d).wait_send()
+        @pl.when(straight(d))
+        def _():
+            z_copy(0, d).wait_send()
+            z_copy(1, d).wait_send()
         return carry
 
     lax.fori_loop(1, NZ - z, drain_z, 0)
+
+    for e in (1, 2):
+        @pl.when((z >= 2) & (z + e < NZ - 1))
+        def _(e=e):
+            forward(0, e).wait_send()
+            forward(1, e).wait_send()
 
     def drain(u, carry):
         w, zz = place(u)
-        for d in (1, 3):
+        for d in (1, 2, 3):
             y_copy(w, zz, d).wait_send()
-        for n in range(2):
-            half_copy(w, zz, n).wait_send()
         c_copy(w, zz).wait_send()
         return carry
 
@@ -430,9 +434,8 @@
             pltpu.VMEM((8, NZ * TILE), jnp.int32),
             dma((5,)),
             dma((NX,)), dma((NX,)),
-            dma((2, NZ)), dma((2, NZ)),
+            dma((2, NZ)), dma((2, NZ)), dma((2, 3)),
             dma((2, NZ, NY)), dma((2, NZ, NY)),
-            dma((2, NZ, 2)), dma((2, NZ, 2)),
             dma((2, NZ)), dma((2, NZ)),
             dma((4,)), dma((4,)), dma((4,)), dma((4,)),
         ],

time: 58.3 us -> 54.1 us (0.928)
  Pallas kernels: 54.7 us -> 51.1 us
    pallas_call x1, Pallas kernels: 54.7 us -> 51.1 us  [shards(): pl.pallas_call(kernel, out_shape=(jax.ShapeDtypeStruct((TOK, HEADS * HEAD...]
where the time goes in v3:
time: 54.1 us; the launch traced here: 54 us
  Pallas kernels  51.1 us (94%)
  local copies, waits for them, and re-layouts  2.27 us (4%)
  between operations  0.65 us (1%)
    pallas_call x1, Pallas kernels, shards(): pl.pallas_call(kernel, out_shape=(jax.ShapeDtypeStruct((TOK, HEADS * HEAD...  51.1 us
    unnamed x4, local copies, waits for them, and re-layouts  2.27 us

profile of v3, /device:TPU:224, one launch (start us, length us, event | category | flops | bytes accessed | tf_op | source)
XLA Modules:
  0.0 54.0 jit_solution(13262726020318206600)
XLA Ops:
  0.6 51.1 %shard_map.68 = (f32[64,1024]{1,0:T(8,128)}, f32[8,64]{1,0:T(8,128)}) custom-call(f32[64,1024]{1,0:T(8,128)} %q_ref.1, f32[64,128]{1,0:T(8,128)} %k_ref.1, f32[64,128]{1,0:T(8,128)} %v_ref.1, s32[512,512]{1,0:T(8,128)} %bm_ref.1, s32[128,128]{1,0:T(8,128)} %bitcast.1), custom_call_target="tpu_custom_call" | custom-call | flops 8589934592 | bytes 4194304 | tf_op jit(solution)/shard_map/pallas_call | solution.py:408
  51.7 0.0 copy-start
  51.7 1.7 %copy.9 = f32[64,1024]{1,0:T(8,128)} copy(f32[64,1024]{1,0:T(8,128)} %get-tuple-element.4) | data formatting | bytes 524288
  53.4 0.0 copy-done
  53.4 0.6 %copy.10 = f32[8,64]{1,0:T(8,128)} copy(f32[8,64]{1,0:T(8,128)S(1)} %copy-done) | data formatting | bytes 4096
Async XLA Ops:
  51.7 1.7 %copy-start = (f32[8,64]{1,0:T(8,128)S(1)}, f32[8,64]{1,0:T(8,128)}, u32[]{:S(2)}) copy-start(f32[8,64]{1,0:T(8,128)} %get-tuple-element.5) | copy-start | bytes 6148

commit v4 on v3

--- a/solution.py
+++ b/solution.py
@@ -64,12 +64,18 @@
         copy.start()
 
     barrier = pltpu.get_barrier_semaphore()
-    peers = [at_x(d) for d in (1, 2, 3)] + [at_y(d) for d in (1, 2, 3)] + [at_z(d) for d in range(1, NZ)] + [partner]
+    peers = [at_x(d) for d in (1, 2, 3)] + [at_y(d) for d in (1, 2, 3)] + [partner]
     for peer in peers:
         pl.semaphore_signal(barrier, inc=1, device_id=peer, device_id_type=MESH)
+
+    def greet(d, carry):
+        pl.semaphore_signal(barrier, inc=1, device_id=at_z(NZ - d), device_id_type=MESH)
+        return carry
+
+    lax.fori_loop(1, z + 1, greet, 0)
     for copy in loads:
         copy.wait()
-    pl.semaphore_wait(barrier, len(peers))
+    pl.semaphore_wait(barrier, len(peers) + NZ - 1 - z)
 
     def remote(ref, send_sem, recv_sem, device, dst=None):
         return pltpu.make_async_remote_copy(

time: 54.1 us -> 54 us (level)
  no operation moved by 1% of the time
where the time goes in v4:
time: 54 us; the launch traced here: 53.9 us
  Pallas kernels  51 us (94%)
  local copies, waits for them, and re-layouts  2.27 us (4%)
  between operations  0.65 us (1%)
    pallas_call x1, Pallas kernels, shards(): pl.pallas_call(kernel, out_shape=(jax.ShapeDtypeStruct((TOK, HEADS * HEAD...  51 us
    unnamed x4, local copies, waits for them, and re-layouts  2.27 us

profile of v4, /device:TPU:224, one launch (start us, length us, event | category | flops | bytes accessed | tf_op | source)
XLA Modules:
  0.0 53.9 jit_solution(1834513398827610398)
XLA Ops:
  0.6 51.0 %shard_map.68 = (f32[64,1024]{1,0:T(8,128)}, f32[8,64]{1,0:T(8,128)}) custom-call(f32[64,1024]{1,0:T(8,128)} %q_ref.1, f32[64,128]{1,0:T(8,128)} %k_ref.1, f32[64,128]{1,0:T(8,128)} %v_ref.1, s32[512,512]{1,0:T(8,128)} %bm_ref.1, s32[128,128]{1,0:T(8,128)} %bitcast.1), custom_call_target="tpu_custom_call" | custom-call | flops 8589934592 | bytes 4194304 | tf_op jit(solution)/shard_map/pallas_call | solution.py:414
  51.6 0.0 copy-start
  51.6 1.7 %copy.9 = f32[64,1024]{1,0:T(8,128)} copy(f32[64,1024]{1,0:T(8,128)} %get-tuple-element.4) | data formatting | bytes 524288
  53.3 0.0 copy-done
  53.3 0.6 %copy.10 = f32[8,64]{1,0:T(8,128)} copy(f32[8,64]{1,0:T(8,128)S(1)} %copy-done) | data formatting | bytes 4096
Async XLA Ops:
  51.6 1.7 %copy-start = (f32[8,64]{1,0:T(8,128)S(1)}, f32[8,64]{1,0:T(8,128)}, u32[]{:S(2)}) copy-start(f32[8,64]{1,0:T(8,128)} %get-tuple-element.5) | copy-start | bytes 6148
